TPU v7x, 256 devices: a whole 4x4x8 slice. The times are simulated.
256 devices in a mesh: dp: 32 (over y, x, core), tensor: 8 (over z).
Axes of the slice: x: 4, y: 4, z: 8, core: 2. Of those that a mesh axis runs over, the one named last changes fastest.
Arguments:
- tokens: bfloat16 [16384, 8192], P(('dp', 'tensor')), may hold values from -6 to 6
- gate_grads: bfloat16 [16384, 28672], P('dp', 'tensor'), may hold values from -6 to 6
- up_grads: bfloat16 [16384, 28672], P('dp', 'tensor'), may hold values from -6 to 6
- input_proj: bfloat16 [8192, 128], replicated, may hold values from -0.0625 to 0.0625
- output_proj: bfloat16 [28672, 128], P('tensor'), may hold values from -0.03125 to 0.03125
- segment_ids: int32 [16384], P('dp'), may hold values from 0 to 3, as said below
- doc_lengths: int32 [128], P('dp'), may hold values from 1 to 256, as said below
- input_inverse: float32 [2, 64, 64], replicated, as said below
- output_inverse: float32 [2, 64, 64], replicated, as said below
- queries: float32 [4096, 8192], P('tensor', 'dp'), may hold values from -0.0625 to 0.0625
Outputs:
- scores: float32 [128, 4096], P('dp', 'tensor')
Inputs may be any that keep to these rules, and one draw needn't show every extreme that they name: `doc_lengths`: within each aligned group of 4 entries (the documents of one index of dp) the lengths sum to 512, and one of them is exactly 256. `segment_ids`: within each aligned group of 512 tokens the ids never fall, and id e appears exactly as often as the e-th length of the group's documents. `input_inverse`: each of the two matrices is symmetric. `output_inverse`: each of the two matrices is symmetric.
All inputs are finite; a program needn't handle non-finite values.
Results may differ from a plain program's by a relative error of at most 0.0003.
Values sent between devices are 32-bit elements; how exact they have to be, the bound alone decides.
A program may use at most 128 MiB of HBM per device.

v0:
```python
import jax
import jax.numpy as jnp
from jax import lax
from jax.sharding import PartitionSpec as P


def outer_sums(left_codes, right_codes, segment_rows, doc_lengths):
    count = doc_lengths.shape[0]
    rows = left_codes.shape[0]
    rank = right_codes.shape[1] // 2
    labels = jnp.arange(count, dtype=jnp.int32)
    member = (segment_rows[:, None] == labels[None, :]).astype(jnp.float32)
    weights = member / doc_lengths.astype(jnp.float32)[None, :]
    spread = weights[:, :, None, None] * left_codes.reshape(rows, 1, 2, rank)
    sums = jnp.einsum(
        "temi,tmj->emij",
        spread,
        right_codes.reshape(rows, 2, rank),
        precision=lax.Precision.HIGHEST,
    )
    return sums.reshape(count, 2 * rank * rank)


def condition(examples, input_inverse, output_inverse):
    count = examples.shape[0]
    rank = input_inverse.shape[1]
    blocks = examples.reshape(count, 2, rank, rank)
    left = jnp.einsum("mik,emkj->emij", input_inverse, blocks, precision=lax.Precision.HIGHEST)
    both = jnp.einsum("emik,mkj->emij", left, output_inverse, precision=lax.Precision.HIGHEST)
    return both.reshape(count, 2 * rank * rank)


def gather_codes(codes_own):
    return lax.all_gather(codes_own, "tensor", axis=0, tiled=True)


def shards(
    tokens,
    gate_grads,
    up_grads,
    input_proj,
    output_proj,
    segment_ids,
    doc_lengths,
    input_inverse,
    output_inverse,
    queries,
):
    rank = input_inverse.shape[1]
    codes_own = jnp.dot(tokens, input_proj, preferred_element_type=jnp.float32)
    grads_part = jnp.concatenate(
        [
            jnp.dot(gate_grads, output_proj[:, :rank], preferred_element_type=jnp.float32),
            jnp.dot(up_grads, output_proj[:, rank:], preferred_element_type=jnp.float32),
        ],
        axis=1,
    )
    grads_full = lax.psum(grads_part, "tensor")
    examples = outer_sums(gather_codes(codes_own), grads_full, segment_ids, doc_lengths)
    conditioned = condition(examples, input_inverse, output_inverse)
    return lax.dot_general(
        conditioned,
        lax.all_gather(queries, "dp", axis=1, tiled=True),
        (((1,), (1,)), ((), ())),
        precision=lax.Precision.HIGHEST,
    )


def solution(mesh):
    return jax.shard_map(
        shards,
        mesh=mesh,
        in_specs=(
            P(("dp", "tensor"), None),
            P("dp", "tensor"),
            P("dp", "tensor"),
            P(),
            P("tensor", None),
            P("dp"),
            P("dp"),
            P(),
            P(),
            P("tensor", "dp"),
        ),
        out_specs=P("dp", "tensor"),
        check_vma=False,
    )
```

profile of v0, /device:TPU:1, one launch (start us, length us, event | category | flops | bytes accessed | tf_op | source)
XLA Modules:
  0.0 131.3 jit_solution(14630794302759269403)
XLA Ops:
  7.4 0.0 copy-start
  7.4 0.0 copy-start.2
  7.4 0.0 all-reduce.2.cloned.1.call-start
  7.4 0.0 copy-start.1
  7.4 4.0 %fusion.1 = f32[512,64]{0,1:T(8,128)S(1)} fusion(bf16[512,3584]{1,0:T(8,128)(2,1)} %param.12, bf16[3584,128]{1,0:T(8,128)(2,1)} %param.14), kind=kOutput, calls=%fused_computation.4 | convolution fusion | flops 234881024 | bytes 4718592 | tf_op jit(solution)/shard_map/dot_general | solution.py:54
  11.4 0.0 copy-done.2
  11.4 0.0 copy-done.1
  11.4 1.2 fusion.3
  12.6 0.0 copy-start.6
  12.6 0.0 copy-start.5
  12.6 0.0 copy-start.3
  12.7 0.0 copy-start.4
  12.7 0.7 pad_maximum_fusion
  13.4 0.0 all-reduce.2.cloned.1.call-update
  13.4 0.0 all-gather.2.cloned.1.call-start
  13.5 0.5 all-gather.2.cloned.1.call-update
  14.0 0.0 copy-done
  14.0 1.7 %fusion.10 = f32[64,128]{1,0:T(8,128)S(1)} fusion(bf16[64,8192]{1,0:T(8,128)(2,1)} %param.10, bf16[8192,128]{1,0:T(8,128)(2,1)S(1)} %copy-done), kind=kOutput, calls=%fused_computation.16 | convolution fusion | flops 134217728 | bytes 3178496 | tf_op jit(solution)/shard_map/dot_general | solution.py:50
  15.7 23.9 %all_gather.6 = f32[512,128]{1,0:T(8,128)S(1)} all-gather(f32[64,128]{1,0:T(8,128)S(1)} %fusion.10), channel_id=1, replica_groups=mesh['dp'=32,'tensor'=8] {'tensor'}, dimensions={0}, use_global_device_ids=true | all-gather | bytes 294912 | tf_op jit(solution)/shard_map/all_gather | solution.py:34
  39.6 0.1 copy.14
  39.7 0.0 copy-done.6
  39.8 0.0 copy-done.5
  39.8 0.1 convert_divide_fusion
  39.8 46.7 %all-reduce.2.cloned.1.call-done = f32[512,2,64]{0,2,1:T(8,128)} async-done(((f32[512,2,64]{0,2,1:T(8,128)}), f32[512,2,64]{0,2,1:T(8,128)}) %all-reduce.2.cloned.1.call-update) | async-done | bytes 262160 | tf_op jit(solution)/shard_map/psum | solution.py:58
  86.5 2.6 %convolution_bitcast_fusion.2 = f32[4,2,64,64]{2,3,0,1:T(8,128)S(1)} fusion(f32[512,2,64]{0,2,1:T(8,128)S(1)} %bitcast.33, f32[512,4]{0,1:T(4,128)S(1)} %convert_divide_fusion, f32[512,2,64]{0,2,1:T(8,128)} %all-reduce.2.cloned.1.call-done), kind=kOutput, calls=%fused_computation.2 | convolution fusion | flops 201588736 | bytes 663552 | tf_op jit(solution)/shard_map/temi,tmj->emij/dot_general | solution.py:15
  89.1 0.0 copy-done.3
  89.1 0.4 convolution_bitcast_fusion.1
  89.5 0.0 copy-done.4
  89.5 0.6 convolution_bitcast_fusion
  90.1 0.1 reshape.43
  90.2 15.9 %all-gather.2.cloned.1.call-done = f32[512,8192]{1,0:T(8,128)} async-done(((f32[512,256]{1,0:T(8,128)}), f32[512,8192]{1,0:T(8,128)}) %all-gather.2.cloned.1.call-update) | async-done | bytes 16777232 | tf_op jit(solution)/shard_map/all_gather | solution.py:63
  106.2 17.7 %fusion.11 = f32[4,512]{1,0:T(4,128)} fusion(f32[4,8192]{1,0:T(4,128)S(1)} %reshape.43, f32[512,8192]{1,0:T(8,128)} %all-gather.2.cloned.1.call-done), kind=kOutput, calls=%fused_computation.17 | convolution fusion | flops 201326592 | bytes 16916480 | tf_op jit(solution)/shard_map/dot_general | solution.py:61
  (2 shorter events, 0.0 us)
Async XLA Ops:
  7.4 6.6 %copy-start = (bf16[8192,128]{1,0:T(8,128)(2,1)S(1)}, bf16[8192,128]{1,0:T(8,128)(2,1)}, u32[]{:S(2)}) copy-start(bf16[8192,128]{1,0:T(8,128)(2,1)} %param.13) | copy-start | bytes 6291460
  7.4 4.0 %copy-start.2 = (bf16[3584,128]{1,0:T(8,128)(2,1)S(1)}, bf16[3584,128]{1,0:T(8,128)(2,1)}, u32[]{:S(2)}) copy-start(bf16[3584,128]{1,0:T(8,128)(2,1)} %param.14) | copy-start | bytes 2752516
  7.4 79.1 %all-reduce.2.cloned.1.call-start = ((), (), s32[]{:S(2)}) async-start(), calls=%async_computation | async-start | bytes 524288 | tf_op jit(solution)/shard_map/psum | solution.py:58
  7.4 4.0 %copy-start.1 = (bf16[512,3584]{1,0:T(8,128)(2,1)S(1)}, bf16[512,3584]{1,0:T(8,128)(2,1)}, u32[]{:S(2)}) copy-start(bf16[512,3584]{1,0:T(8,128)(2,1)} %param.11) | copy-start | bytes 11010052
  12.6 27.1 %copy-start.6 = (s32[4]{0:T(128)S(1)}, s32[4]{0:T(128)}, u32[]{:S(2)}) copy-start(s32[4]{0:T(128)} %param.16) | copy-start | bytes 52
  12.6 27.1 %copy-start.5 = (s32[512]{0:T(512)S(1)}, s32[512]{0:T(512)}, u32[]{:S(2)}) copy-start(s32[512]{0:T(512)} %param.15) | copy-start | bytes 6148
  12.6 76.4 %copy-start.3 = (f32[2,64,64]{2,1,0:T(8,128)S(1)}, f32[2,64,64]{2,1,0:T(8,128)}, u32[]{:S(2)}) copy-start(f32[2,64,64]{2,1,0:T(8,128)} %param.17) | copy-start | bytes 98308
  12.7 76.8 %copy-start.4 = (f32[2,64,64]{2,1,0:T(8,128)S(1)}, f32[2,64,64]{2,1,0:T(8,128)}, u32[]{:S(2)}) copy-start(f32[2,64,64]{2,1,0:T(8,128)} %param.18) | copy-start | bytes 98308
  13.4 92.8 %all-gather.2.cloned.1.call-start = ((), (), s32[]{:S(2)}) async-start(), calls=%async_computation.1 | async-start | bytes 17301504 | tf_op jit(solution)/shard_map/all_gather | solution.py:63
Sparse Core Ops, SparseCore 0:
  13.5 72.9 all-reduce.1
Sparse Core Ops, SparseCore 1:
  16.7 89.5 all-gather.1
where the time goes:
time: 131 us
  waiting for transfers between devices  63.1 us (48%)
  matrix products  28.2 us (22%)
  blocking collectives  23.9 us (18%)
  between operations  15 us (11%)
    psum x1, waiting for transfers between devices, shards(): grads_full = lax.psum(grads_part, 'tensor')  46.7 us
    all_gather x1, blocking collectives, gather_codes(): return lax.all_gather(codes_own, 'tensor', axis=0, tiled=True)  23.9 us
    dot_general x1, matrix products, shards(): lax.dot_general(conditioned, lax.all_gather(queries, 'dp', axis=1, tiled=...  17.7 us
    all_gather x1, waiting for transfers between devices, shards(): lax.all_gather(queries, 'dp', axis=1, tiled=True)  15.9 us
    dot_general x1, matrix products, shards(): jnp.dot(up_grads, output_proj[:, rank:], preferred_element_type=jnp.float32)  3.98 us
  transfers between devices with their start and end apart: 2, of which 2 were waited for; matrix products, arithmetic and copies ran while one was open for 4% of the time, Pallas kernels for 0%

commit v1 on v0

v1 whole, which is shorter than its diff:
```python
import jax
import jax.numpy as jnp
from jax import lax
from jax.experimental import pallas as pl
from jax.experimental.pallas import tpu as pltpu
from jax.sharding import PartitionSpec as P

F32, BF16 = jnp.float32, jnp.bfloat16
FAR_FIRST = (4, 3, 5, 2, 6, 1, 7)
PEERS = ((2, 1), (2, 0), (1, 1), (3, 1), (1, 0), (3, 0), (0, 1))
CHUNKS = 2
NN = (((1,), (0,)), ((), ()))
NT = (((1,), (1,)), ((), ()))


def mm(a, b, dims):
    return lax.dot_general(a, b, dims, preferred_element_type=F32)


def exact(a, b, dims):
    return lax.dot_general(a, b, dims, precision=lax.Precision.HIGHEST, preferred_element_type=F32)


def split(a):
    hi = a.astype(BF16)
    return hi, (a - hi.astype(F32)).astype(BF16)


def mm3(a, b, dims):
    (ah, al), (bh, bl) = a, b
    return mm(ah, bh, dims) + (mm(ah, bl, dims) + mm(al, bh, dims))


def iota(shape, axis):
    return lax.broadcasted_iota(jnp.int32, shape, axis)


def kernel(
    tokens_hbm, gate_hbm, up_hbm, iproj_hbm, oproj_hbm, seg_hbm, len_hbm, ainv_hbm, binv_hbm, query_hbm,
    out_ref,
    tokens, gate, up, iproj, oproj, seg, lens, ainv, binv, query,
    csend, cbuf, gsend, gbuf, qbuf, qhi, qlo, esend, ebuf, rsum, psend, pbuf,
    load_sem, c_sem, g_send, g_recv, q_send, q_recv, e_sem, p_sem, ready,
):
    d, z = lax.axis_index("dp"), lax.axis_index("tensor")
    y, x, c = d // 8, lax.rem(d // 2, 4), lax.rem(d, 2)
    m, jz = z // 4, lax.rem(z, 4)

    def dp(y_to, x_to, c_to):
        return lax.rem(y_to, 4) * 8 + lax.rem(x_to, 4) * 2 + lax.rem(c_to, 2)

    def ring(k):
        return lax.rem(z + k, 8)

    def send(src, dst, s_sem, r_sem, to):
        copy = pltpu.make_async_remote_copy(
            src_ref=src, dst_ref=dst, send_sem=s_sem, recv_sem=r_sem, device_id=to, device_id_type=pl.DeviceIdType.MESH
        )
        copy.start()

    def took(ref, sem):
        pltpu.make_async_copy(ref, ref, sem).wait()

    left, right = (dp(y, x + 3, c), z), (dp(y, x + 1, c), z)
    peers = [(dp(y + ky, x, c + kc), z) for ky, kc in PEERS]

    tc = gate.shape[0] // CHUNKS
    rows = [pl.ds(n * tc, tc) for n in range(CHUNKS)]
    pairs = [(tokens_hbm, tokens), (iproj_hbm, iproj), (ainv_hbm, ainv), (query_hbm, query), (binv_hbm, binv),
             (oproj_hbm, oproj), (seg_hbm, seg), (len_hbm, lens)]
    for n in range(CHUNKS):
        pairs += [(gate_hbm.at[rows[n]], gate.at[rows[n]]), (up_hbm.at[rows[n]], up.at[rows[n]])]
    loads = [pltpu.make_async_copy(src, dst, load_sem.at[i]) for i, (src, dst) in enumerate(pairs)]
    for load in loads:
        load.start()

    barrier = pltpu.get_barrier_semaphore()
    greet = [(d, ring(k)) for k in FAR_FIRST] + peers + [left, right]
    for to in greet:
        pl.semaphore_signal(barrier, inc=1, device_id=to, device_id_type=pl.DeviceIdType.MESH)

    loads[0].wait()
    loads[1].wait()
    codes = mm(tokens[...], iproj[...], NN)
    loads[2].wait()
    r, i = iota((64, 64), 0), iota((64, 64), 1)
    source = (((r >> 2) & 1) << 5) + ((r & 1) << 4) + (((r >> 5) & 1) << 3) + (((r >> 1) & 1) << 2) + ((r >> 3) & 3)
    order = (source == i).astype(F32)
    halves = [(iota((64, 128), 1) == iota((64, 128), 0) + 64 * n).astype(F32) for n in range(2)]
    left_inverse = jnp.concatenate(
        [exact(exact(order, ainv[n], NN), halves[n], NN) for n in range(2)], axis=0
    )
    both = mm3(split(left_inverse), split(jnp.concatenate([codes, codes], axis=0)), NT)
    low = iota((32, 128), 1) < 64
    for n in range(2):
        csend[n] = jnp.where(low, both[64 * n : 64 * n + 32], both[64 * n + 32 : 64 * n + 64])

    loads[3].wait()
    r, i = iota((256, 256), 0), iota((256, 256), 1)
    shuffle = ((((r >> 4) & 3) << 6) + ((r >> 6) << 4) + (r & 15) == i).astype(BF16)
    q_hi, q_lo = split(query[...])
    qbuf[x] = mm(shuffle, q_hi, NT) + mm(shuffle, q_lo, NT)

    loads[4].wait()
    right_inverse = split(jnp.concatenate([exact(binv[n], halves[n], NN) for n in range(2)], axis=0))

    pl.semaphore_wait(barrier, len(greet))

    for k in FAR_FIRST:
        send(csend.at[ring(k) // 4], cbuf.at[z], c_sem.at[0], c_sem.at[1], (d, ring(k)))
    for to in peers:
        pl.semaphore_signal(ready, inc=1, device_id=to, device_id_type=pl.DeviceIdType.MESH)
    first, second = pl.ds(0, 128), pl.ds(128, 128)
    send(qbuf.at[x, first], qbuf.at[x, first], q_send.at[0], q_recv.at[0], left)
    send(qbuf.at[x, second], qbuf.at[x, second], q_send.at[1], q_recv.at[1], right)
    send(qbuf.at[x, second], qbuf.at[x, second], q_send.at[2], q_recv.at[2], left)
    send(qbuf.at[x, first], qbuf.at[x, first], q_send.at[3], q_recv.at[3], right)
    cbuf[z] = csend[m]

    loads[5].wait()
    low = iota((tc, 128), 1) < 64
    for n in range(CHUNKS):
        loads[8 + 2 * n].wait()
        part = mm(gate[rows[n]], oproj[...], NN)
        loads[9 + 2 * n].wait()
        part = jnp.where(low, part, mm(up[rows[n]], oproj[...], NN))
        gsend[n] = mm3(right_inverse, split(part), NT).reshape(8, 16, tc)
        for k in FAR_FIRST:
            send(gsend.at[n, ring(k)], gbuf.at[n, k - 1], g_send.at[n], g_recv.at[n], (d, ring(k)))

    loads[6].wait()
    loads[7].wait()
    weights = [
        jnp.where(seg[...] == g, 1.0 / jnp.broadcast_to(lens[:, g : g + 1], seg.shape).astype(F32), 0.0) for g in range(4)
    ]

    took(cbuf.at[pl.ds(0, 7)], c_sem.at[1])
    low = iota((32, 128), 1) < 64
    upper, lower = [], []
    for n in range(4):
        even, odd = cbuf[2 * n], cbuf[2 * n + 1]
        upper.append(jnp.where(low, even, pltpu.roll(odd, 64, 1)))
        lower.append(jnp.where(low, pltpu.roll(even, 64, 1), odd))
    codes_t = split(jnp.concatenate([jnp.concatenate(upper, axis=1), jnp.concatenate(lower, axis=1)], axis=0))

    took(qbuf.at[0, first], q_recv.at[0])
    after = lax.rem(x + 1, 4)
    send(qbuf.at[after, first], qbuf.at[after, first], q_send.at[4], q_recv.at[4], left)
    took(qbuf.at[0, first], q_recv.at[1])
    before = lax.rem(x + 3, 4)
    send(qbuf.at[before, second], qbuf.at[before, second], q_send.at[5], q_recv.at[5], right)

    sums = []
    for n in range(CHUNKS):
        took(gbuf.at[n], g_recv.at[n])
        total = gsend[n, z]
        for k in range(7):
            total = total + gbuf[n, k]
        sums.append(total)
    columns = jnp.concatenate(sums, axis=1)
    spread = jnp.concatenate([columns * w for w in weights] * 2, axis=0)
    outer = mm3(codes_t, split(spread), NT)
    turned = [outer] + [pltpu.roll(outer, 16 * k, 1) for k in (1, 2, 3)]
    place = iota((8, 128), 1) >> 4
    for g in range(4):
        piece = turned[(0 - g) % 4][0:8]
        for k in range(1, 8):
            piece = jnp.where(place == k, turned[(k - g) % 4][8 * k : 8 * k + 8], piece)
        esend[pl.ds(g, 8, stride=4), :] = piece

    pl.semaphore_wait(ready, len(peers))
    mine = [[(y == 2 * m + ky) & (c == kc) for kc in range(2)] for ky in range(2)]
    for k in FAR_FIRST + (0,):
        for ky in range(2):
            for kc in range(2):
                y_to, src = 2 * m + ky, esend.at[pl.ds(8 * (2 * ky + kc), 8)]
                slot = (lax.rem(y - y_to + 4, 4) * 2 + lax.rem(c + kc, 2)) * 4 + jz
                dst = ebuf.at[slot]
                to = (dp(y_to, x, kc), ring(k))
                if k:
                    send(src, dst, e_sem.at[0], e_sem.at[1], to)
                else:

                    @pl.when(jnp.logical_not(mine[ky][kc]))
                    def _(src=src, dst=dst, to=to):
                        send(src, dst, e_sem.at[0], e_sem.at[1], to)

                    @pl.when(mine[ky][kc])
                    def _(src=src, dst=dst):
                        pltpu.make_async_copy(src, dst, e_sem.at[1]).start()

    def prepare(block, jzs):
        for n in jzs:
            hi, lo = split(qbuf[block, pl.ds(64 * n, 64)])
            at = pl.ds(pl.multiple_of(lax.rem(block, 2) * 64, 64), 64)
            qhi[block // 2, n, at] = hi
            qlo[block // 2, n, at] = lo

    prepare(x, range(4))
    prepare(after, range(2))
    prepare(before, range(2, 4))
    took(qbuf.at[0, first], q_recv.at[2])
    prepare(after, range(2, 4))
    took(qbuf.at[0, first], q_recv.at[3])
    prepare(before, range(2))
    beyond = lax.rem(x + 2, 4)
    took(qbuf.at[0, first], q_recv.at[4])
    prepare(beyond, range(2))
    took(qbuf.at[0, first], q_recv.at[5])
    prepare(beyond, range(2, 4))

    took(ebuf, e_sem.at[1])
    pieces = ebuf[...].reshape(8, 4, 8, 128)
    e_hi, e_lo = split(jnp.concatenate([pieces[:, n].reshape(64, 128) for n in range(4)], axis=1))
    e_both = jnp.concatenate([e_hi, e_lo], axis=0)
    part = []
    for n in range(2):
        main = mm(e_both, qhi[n].reshape(512, 512), NN)
        part.append(main[:64] + main[64:] + mm(e_hi, qlo[n].reshape(512, 512), NN))
    rsum[...] = part[1]
    for n in range(8):
        psend[n] = part[0][8 * n : 8 * n + 4] + rsum[8 * n + 4 : 8 * n + 8]
    for (ky, kc), to in zip(PEERS, peers, strict=True):
        n = 2 * ky + kc
        send(psend.at[n], pbuf.at[n - 1], p_sem.at[0], p_sem.at[1], to)
    took(pbuf, p_sem.at[1])
    total = psend[0]
    for n in range(7):
        total = total + pbuf[n]
    out_ref[...] = total

    took(cbuf.at[pl.ds(0, 7)], c_sem.at[0])
    for n in range(CHUNKS):
        took(gbuf.at[n], g_send.at[n])
    for n in range(6):
        took(qbuf.at[0, first], q_send.at[n])
    took(ebuf.at[pl.ds(0, 31)], e_sem.at[0])

    @pl.when(m != y // 2)
    def _():
        took(ebuf.at[0], e_sem.at[0])

    took(pbuf, p_sem.at[0])


def shards(*args):
    tokens, gate, up, iproj, oproj, seg, lens, ainv, binv, query = args
    tc = gate.shape[0] // CHUNKS
    dma, vmem = pltpu.SemaphoreType.DMA, pltpu.VMEM
    return pl.pallas_call(
        kernel,
        out_shape=jax.ShapeDtypeStruct((4, 512), F32),
        in_specs=[pl.BlockSpec(memory_space=pl.ANY)] * 10,
        out_specs=pl.BlockSpec(memory_space=pltpu.VMEM),
        scratch_shapes=[
            vmem(tokens.shape, BF16),
            vmem(gate.shape, BF16),
            vmem(up.shape, BF16),
            vmem(iproj.shape, BF16),
            vmem(oproj.shape, BF16),
            vmem((1, 512), jnp.int32),
            vmem((1, 4), jnp.int32),
            vmem(ainv.shape, F32),
            vmem(binv.shape, F32),
            vmem(query.shape, F32),
            vmem((2, 32, 128), F32),
            vmem((8, 32, 128), F32),
            vmem((CHUNKS, 8, 16, tc), F32),
            vmem((CHUNKS, 7, 16, tc), F32),
            vmem((4, 256, 512), F32),
            vmem((2, 4, 128, 512), BF16),
            vmem((2, 4, 128, 512), BF16),
            vmem((32, 128), F32),
            vmem((32, 8, 128), F32),
            vmem((64, 512), F32),
            vmem((8, 4, 512), F32),
            vmem((7, 4, 512), F32),
            dma((8 + 2 * CHUNKS,)),
            dma((2,)),
            dma((CHUNKS,)),
            dma((CHUNKS,)),
            dma((6,)),
            dma((6,)),
            dma((2,)),
            dma((2,)),
            pltpu.SemaphoreType.REGULAR,
        ],
        compiler_params=pltpu.CompilerParams(
            collective_id=0, has_side_effects=True, vmem_limit_bytes=56 * 2**20
        ),
        cost_estimate=pl.CostEstimate(flops=10**9, bytes_accessed=12 * 10**6, transcendentals=0),
    )(tokens, gate, up, iproj, oproj, seg.reshape(1, 512), lens.reshape(1, 4), ainv, binv, query)


def solution(mesh):
    return jax.shard_map(
        shards,
        mesh=mesh,
        in_specs=(
            P(("dp", "tensor"), None),
            P("dp", "tensor"),
            P("dp", "tensor"),
            P(),
            P("tensor", None),
            P("dp"),
            P("dp"),
            P(),
            P(),
            P("tensor", "dp"),
        ),
        out_specs=P("dp", "tensor"),
        check_vma=False,
    )
```

time: 131 us -> 35.9 us (0.27)
  waiting for transfers between devices: 63.1 us -> 0 us
  Pallas kernels: 0 us -> 34.4 us
  matrix products: 28.2 us -> 0 us
  blocking collectives: 23.9 us -> 0 us
  between operations: 15 us -> 0.01 us
    psum x1 -> x0, waiting for transfers between devices: 46.7 us -> none  [shards(): grads_full = lax.psum(grads_part, 'tensor')]
    pallas_call x0 -> x1, Pallas kernels: none -> 34.4 us  [shards(): pl.pallas_call(kernel, out_shape=jax.ShapeDtypeStruct((4, 512), F32), in_...]
    dot_general x7 -> x0, matrix products: 28.2 us -> none  [the longest x1 17.7 us: shards(): lax.dot_general(conditioned, lax.all_gather(queries, 'dp', axis=1, tiled=...]
    all_gather x1 -> x0, blocking collectives: 23.9 us -> none  [gather_codes(): return lax.all_gather(codes_own, 'tensor', axis=0, tiled=True)]
    all_gather x1 -> x0, waiting for transfers between devices: 15.9 us -> none  [shards(): lax.all_gather(queries, 'dp', axis=1, tiled=True)]
  transfers between devices with their start and end apart: 2 -> 0, of which waited for: 2 -> 0; matrix products, arithmetic and copies ran while one was open for 4% -> 0% of each run, Pallas kernels for 0% -> 0%
where the time goes in v1:
time: 35.9 us; the launch traced here: 35.7 us
  Pallas kernels  34.4 us (96%)
  local copies, waits for them, and re-layouts  1.3 us (4%)
    pallas_call x1, Pallas kernels, shards(): pl.pallas_call(kernel, out_shape=jax.ShapeDtypeStruct((4, 512), F32), in_...  34.4 us
    unnamed x1, local copies, waits for them, and re-layouts  1.3 us

profile of v1, /device:TPU:1, one launch (start us, length us, event | category | flops | bytes accessed | tf_op | source)
XLA Modules:
  0.0 35.7 jit_solution(1429093783253148080)
XLA Ops:
  0.0 34.4 %shard_map.100 = f32[4,512]{1,0:T(4,128)} custom-call(bf16[64,8192]{1,0:T(8,128)(2,1)} %tokens_hbm.1, bf16[512,3584]{1,0:T(8,128)(2,1)} %gate_hbm.1, bf16[512,3584]{1,0:T(8,128)(2,1)} %up_hbm.1, bf16[8192,128]{1,0:T(8,128)(2,1)} %iproj_hbm.1, bf16[3584,128]{1,0:T(8,128)(2,1)} %oproj_hbm.1, s32[1,512]{1,0:T(1,128)} %bitcast.2, s32[1,4]{1,0:T(1,128)} %bitcast.3, ...), custom_call_target="tpu_custom_call" | custom-call | flops 1000000000 | bytes 12000000 | tf_op jit(solution)/shard_map/pallas_call | solution.py:250
  34.4 1.3 %copy.12 = f32[4,512]{1,0:T(4,128)} copy(f32[4,512]{1,0:T(4,128)} %shard_map.100) | data formatting | bytes 16384

commit v2 on v1

--- a/solution.py
+++ b/solution.py
@@ -40,7 +40,7 @@
     out_ref,
     tokens, gate, up, iproj, oproj, seg, lens, ainv, binv, query,
     csend, cbuf, gsend, gbuf, qbuf, qhi, qlo, esend, ebuf, rsum, psend, pbuf,
-    load_sem, c_sem, g_send, g_recv, q_send, q_recv, e_sem, p_sem, ready,
+    load_sem, c_sem, g_send, g_recv, q_send, q_recv, e_sem, p_sem, told, ready,
 ):
     d, z = lax.axis_index("dp"), lax.axis_index("tensor")
     y, x, c = d // 8, lax.rem(d // 2, 4), lax.rem(d, 2)
@@ -66,7 +66,7 @@
 
     tc = gate.shape[0] // CHUNKS
     rows = [pl.ds(n * tc, tc) for n in range(CHUNKS)]
-    pairs = [(tokens_hbm, tokens), (iproj_hbm, iproj), (ainv_hbm, ainv), (query_hbm, query), (binv_hbm, binv),
+    pairs = [(query_hbm, query), (ainv_hbm, ainv), (binv_hbm, binv), (tokens_hbm, tokens), (iproj_hbm, iproj),
              (oproj_hbm, oproj), (seg_hbm, seg), (len_hbm, lens)]
     for n in range(CHUNKS):
         pairs += [(gate_hbm.at[rows[n]], gate.at[rows[n]]), (up_hbm.at[rows[n]], up.at[rows[n]])]
@@ -75,47 +75,63 @@
         load.start()
 
     barrier = pltpu.get_barrier_semaphore()
-    greet = [(d, ring(k)) for k in FAR_FIRST] + peers + [left, right]
+    pair = (dp(y, x, c + 1), z)
+    greet = [(dp(y, x, 0), ring(k)) for k in FAR_FIRST]
+    greet += [(dp(y + k, x, 0), z) for k in (2, 1, 3)]
+    greet += [(dp(y, x + k, 1), z) for k in (1, 3)] + [pair]
+
+    def signal(sem, to):
+        pl.semaphore_signal(sem, inc=1, device_id=to, device_id_type=pl.DeviceIdType.MESH)
+
+    def learn(core, count):
+        @pl.when(c == core)
+        def _():
+            pl.semaphore_wait(barrier, count)
+            signal(told, pair)
+
+        @pl.when(c != core)
+        def _():
+            pl.semaphore_wait(told, 1)
+
     for to in greet:
-        pl.semaphore_signal(barrier, inc=1, device_id=to, device_id_type=pl.DeviceIdType.MESH)
-
-    loads[0].wait()
+        signal(barrier, to)
+
     loads[1].wait()
-    codes = mm(tokens[...], iproj[...], NN)
-    loads[2].wait()
     r, i = iota((64, 64), 0), iota((64, 64), 1)
     source = (((r >> 2) & 1) << 5) + ((r & 1) << 4) + (((r >> 5) & 1) << 3) + (((r >> 1) & 1) << 2) + ((r >> 3) & 3)
     order = (source == i).astype(F32)
     halves = [(iota((64, 128), 1) == iota((64, 128), 0) + 64 * n).astype(F32) for n in range(2)]
-    left_inverse = jnp.concatenate(
-        [exact(exact(order, ainv[n], NN), halves[n], NN) for n in range(2)], axis=0
+    left_inverse = split(
+        jnp.concatenate([exact(exact(order, ainv[n], NN), halves[n], NN) for n in range(2)], axis=0)
     )
-    both = mm3(split(left_inverse), split(jnp.concatenate([codes, codes], axis=0)), NT)
+    loads[2].wait()
+    right_inverse = split(jnp.concatenate([exact(binv[n], halves[n], NN) for n in range(2)], axis=0))
+
+    loads[3].wait()
+    loads[4].wait()
+    codes = mm(tokens[...], iproj[...], NN)
+    both = mm3(left_inverse, split(jnp.concatenate([codes, codes], axis=0)), NT)
     low = iota((32, 128), 1) < 64
     for n in range(2):
         csend[n] = jnp.where(low, both[64 * n : 64 * n + 32], both[64 * n + 32 : 64 * n + 64])
-
-    loads[3].wait()
+    cbuf[z] = csend[m]
+
     r, i = iota((256, 256), 0), iota((256, 256), 1)
     shuffle = ((((r >> 4) & 3) << 6) + ((r >> 6) << 4) + (r & 15) == i).astype(BF16)
+    loads[0].wait()
     q_hi, q_lo = split(query[...])
     qbuf[x] = mm(shuffle, q_hi, NT) + mm(shuffle, q_lo, NT)
 
-    loads[4].wait()
-    right_inverse = split(jnp.concatenate([exact(binv[n], halves[n], NN) for n in range(2)], axis=0))
-
-    pl.semaphore_wait(barrier, len(greet))
-
-    for k in FAR_FIRST:
-        send(csend.at[ring(k) // 4], cbuf.at[z], c_sem.at[0], c_sem.at[1], (d, ring(k)))
-    for to in peers:
-        pl.semaphore_signal(ready, inc=1, device_id=to, device_id_type=pl.DeviceIdType.MESH)
+    learn(1, 5)
     first, second = pl.ds(0, 128), pl.ds(128, 128)
     send(qbuf.at[x, first], qbuf.at[x, first], q_send.at[0], q_recv.at[0], left)
     send(qbuf.at[x, second], qbuf.at[x, second], q_send.at[1], q_recv.at[1], right)
     send(qbuf.at[x, second], qbuf.at[x, second], q_send.at[2], q_recv.at[2], left)
     send(qbuf.at[x, first], qbuf.at[x, first], q_send.at[3], q_recv.at[3], right)
-    cbuf[z] = csend[m]
+
+    learn(0, 21)
+    for k in FAR_FIRST:
+        send(csend.at[ring(k) // 4], cbuf.at[z], c_sem.at[0], c_sem.at[1], (d, ring(k)))
 
     loads[5].wait()
     low = iota((tc, 128), 1) < 64
@@ -127,6 +143,9 @@
         gsend[n] = mm3(right_inverse, split(part), NT).reshape(8, 16, tc)
         for k in FAR_FIRST:
             send(gsend.at[n, ring(k)], gbuf.at[n, k - 1], g_send.at[n], g_recv.at[n], (d, ring(k)))
+
+    for to in peers:
+        signal(ready, to)
 
     loads[6].wait()
     loads[7].wait()
@@ -284,6 +303,7 @@
             dma((2,)),
             dma((2,)),
             pltpu.SemaphoreType.REGULAR,
+            pltpu.SemaphoreType.REGULAR,
         ],
         compiler_params=pltpu.CompilerParams(
             collective_id=0, has_side_effects=True, vmem_limit_bytes=56 * 2**20

time: 35.9 us -> 33.4 us (0.930)
  Pallas kernels: 34.4 us -> 32 us
    pallas_call x1, Pallas kernels: 34.4 us -> 32 us  [shards(): pl.pallas_call(kernel, out_shape=jax.ShapeDtypeStruct((4, 512), F32), in_...]
where the time goes in v2:
time: 33.4 us; the launch traced here: 33.3 us
  Pallas kernels  32 us (96%)
  local copies, waits for them, and re-layouts  1.3 us (4%)
    pallas_call x1, Pallas kernels, shards(): pl.pallas_call(kernel, out_shape=jax.ShapeDtypeStruct((4, 512), F32), in_...  32 us
    unnamed x1, local copies, waits for them, and re-layouts  1.3 us

profile of v2, /device:TPU:1, one launch (start us, length us, event | category | flops | bytes accessed | tf_op | source)
XLA Modules:
  0.0 33.3 jit_solution(12284086316482257985)
XLA Ops:
  0.0 32.0 %shard_map.100 = f32[4,512]{1,0:T(4,128)} custom-call(bf16[64,8192]{1,0:T(8,128)(2,1)} %tokens_hbm.1, bf16[512,3584]{1,0:T(8,128)(2,1)} %gate_hbm.1, bf16[512,3584]{1,0:T(8,128)(2,1)} %up_hbm.1, bf16[8192,128]{1,0:T(8,128)(2,1)} %iproj_hbm.1, bf16[3584,128]{1,0:T(8,128)(2,1)} %oproj_hbm.1, s32[1,512]{1,0:T(1,128)} %bitcast.2, s32[1,4]{1,0:T(1,128)} %bitcast.3, ...), custom_call_target="tpu_custom_call" | custom-call | flops 1000000000 | bytes 12000000 | tf_op jit(solution)/shard_map/pallas_call | solution.py:269
  32.0 1.3 %copy.12 = f32[4,512]{1,0:T(4,128)} copy(f32[4,512]{1,0:T(4,128)} %shard_map.100) | data formatting | bytes 16384

commit v3 on v2

--- a/solution.py
+++ b/solution.py
@@ -66,13 +66,10 @@
 
     tc = gate.shape[0] // CHUNKS
     rows = [pl.ds(n * tc, tc) for n in range(CHUNKS)]
-    pairs = [(query_hbm, query), (ainv_hbm, ainv), (binv_hbm, binv), (tokens_hbm, tokens), (iproj_hbm, iproj),
-             (oproj_hbm, oproj), (seg_hbm, seg), (len_hbm, lens)]
-    for n in range(CHUNKS):
-        pairs += [(gate_hbm.at[rows[n]], gate.at[rows[n]]), (up_hbm.at[rows[n]], up.at[rows[n]])]
+    pairs = [(query_hbm, query), (ainv_hbm, ainv), (binv_hbm, binv), (tokens_hbm, tokens), (iproj_hbm, iproj), (oproj_hbm, oproj), (seg_hbm, seg), (len_hbm, lens), (gate_hbm.at[rows[0]], gate.at[rows[0]]), (up_hbm.at[rows[0]], up.at[rows[0]]), (gate_hbm.at[rows[1]], gate.at[rows[1]]), (up_hbm.at[rows[1]], up.at[rows[1]])]
     loads = [pltpu.make_async_copy(src, dst, load_sem.at[i]) for i, (src, dst) in enumerate(pairs)]
-    for load in loads:
-        load.start()
+    for i in (0, 1, 2, 3, 4, 5, 6, 7, 8, 9, 10, 11):
+        loads[i].start()
 
     barrier = pltpu.get_barrier_semaphore()
     pair = (dp(y, x, c + 1), z)
@@ -189,24 +186,21 @@
 
     pl.semaphore_wait(ready, len(peers))
     mine = [[(y == 2 * m + ky) & (c == kc) for kc in range(2)] for ky in range(2)]
-    for k in FAR_FIRST + (0,):
+    for zt in (0, 1, 2, 3, 7, 4, 6, 5):
         for ky in range(2):
             for kc in range(2):
                 y_to, src = 2 * m + ky, esend.at[pl.ds(8 * (2 * ky + kc), 8)]
                 slot = (lax.rem(y - y_to + 4, 4) * 2 + lax.rem(c + kc, 2)) * 4 + jz
                 dst = ebuf.at[slot]
-                to = (dp(y_to, x, kc), ring(k))
-                if k:
+                own = mine[ky][kc] & (z == zt)
+
+                @pl.when(jnp.logical_not(own))
+                def _(src=src, dst=dst, to=(dp(y_to, x, kc), zt)):
                     send(src, dst, e_sem.at[0], e_sem.at[1], to)
-                else:
-
-                    @pl.when(jnp.logical_not(mine[ky][kc]))
-                    def _(src=src, dst=dst, to=to):
-                        send(src, dst, e_sem.at[0], e_sem.at[1], to)
-
-                    @pl.when(mine[ky][kc])
-                    def _(src=src, dst=dst):
-                        pltpu.make_async_copy(src, dst, e_sem.at[1]).start()
+
+                @pl.when(own)
+                def _(src=src, dst=dst):
+                    pltpu.make_async_copy(src, dst, e_sem.at[1]).start()
 
     def prepare(block, jzs):
         for n in jzs:
@@ -268,7 +262,7 @@
     dma, vmem = pltpu.SemaphoreType.DMA, pltpu.VMEM
     return pl.pallas_call(
         kernel,
-        out_shape=jax.ShapeDtypeStruct((4, 512), F32),
+        out_shape=pltpu.VMEM((4, 512), F32),
         in_specs=[pl.BlockSpec(memory_space=pl.ANY)] * 10,
         out_specs=pl.BlockSpec(memory_space=pltpu.VMEM),
         scratch_shapes=[

time: 33.4 us -> 31.8 us (0.952)
  Pallas kernels: 32 us -> 31.2 us
  local copies, waits for them, and re-layouts: 1.3 us -> 0.6 us
    pallas_call x1, Pallas kernels: 32 us -> 31.2 us  [shards(): pl.pallas_call(kernel, out_shape=pltpu.VMEM((4, 512), F32), in_specs=[pl....]
    unnamed x1, local copies, waits for them, and re-layouts: 1.3 us -> 0.6 us
where the time goes in v3:
time: 31.8 us
  Pallas kernels  31.2 us (98%)
  local copies, waits for them, and re-layouts  0.6 us (2%)
    pallas_call x1, Pallas kernels, shards(): pl.pallas_call(kernel, out_shape=pltpu.VMEM((4, 512), F32), in_specs=[pl....  31.2 us

profile of v3, /device:TPU:1, one launch (start us, length us, event | category | flops | bytes accessed | tf_op | source)
XLA Modules:
  0.0 31.8 jit_solution(833398866015585007)
XLA Ops:
  0.0 31.2 %shard_map.100 = f32[4,512]{1,0:T(4,128)S(1)} custom-call(bf16[64,8192]{1,0:T(8,128)(2,1)} %tokens_hbm.1, bf16[512,3584]{1,0:T(8,128)(2,1)} %gate_hbm.1, bf16[512,3584]{1,0:T(8,128)(2,1)} %up_hbm.1, bf16[8192,128]{1,0:T(8,128)(2,1)} %iproj_hbm.1, bf16[3584,128]{1,0:T(8,128)(2,1)} %oproj_hbm.1, s32[1,512]{1,0:T(1,128)} %bitcast.2, s32[1,4]{1,0:T(1,128)} %bitcast.3, ...), custom_call_target="tpu_custom_call" | custom-call | flops 1000000000 | bytes 12000000 | tf_op jit(solution)/shard_map/pallas_call | solution.py:263
  31.2 0.6 %copy.12 = f32[4,512]{1,0:T(4,128)} copy(f32[4,512]{1,0:T(4,128)S(1)} %shard_map.100) | data formatting | bytes 16384

commit v4 on v2

--- a/solution.py
+++ b/solution.py
@@ -7,7 +7,7 @@
 
 F32, BF16 = jnp.float32, jnp.bfloat16
 FAR_FIRST = (4, 3, 5, 2, 6, 1, 7)
-PEERS = ((2, 1), (2, 0), (1, 1), (3, 1), (1, 0), (3, 0), (0, 1))
+PEERS = (2, 1, 3)
 CHUNKS = 2
 NN = (((1,), (0,)), ((), ()))
 NT = (((1,), (1,)), ((), ()))
@@ -62,7 +62,7 @@
         pltpu.make_async_copy(ref, ref, sem).wait()
 
     left, right = (dp(y, x + 3, c), z), (dp(y, x + 1, c), z)
-    peers = [(dp(y + ky, x, c + kc), z) for ky, kc in PEERS]
+    peers = [(dp(y + k, x, c), z) for k in PEERS]
 
     tc = gate.shape[0] // CHUNKS
     rows = [pl.ds(n * tc, tc) for n in range(CHUNKS)]
@@ -76,9 +76,9 @@
 
     barrier = pltpu.get_barrier_semaphore()
     pair = (dp(y, x, c + 1), z)
-    greet = [(dp(y, x, 0), ring(k)) for k in FAR_FIRST]
-    greet += [(dp(y + k, x, 0), z) for k in (2, 1, 3)]
-    greet += [(dp(y, x + k, 1), z) for k in (1, 3)] + [pair]
+    greet = [(dp(y, x, 1), ring(k)) for k in FAR_FIRST]
+    greet += [(dp(y + k, x, 1), z) for k in PEERS]
+    greet += [(dp(y, x + k, 0), z) for k in (1, 3)] + [pair]
 
     def signal(sem, to):
         pl.semaphore_signal(sem, inc=1, device_id=to, device_id_type=pl.DeviceIdType.MESH)
@@ -96,9 +96,37 @@
     for to in greet:
         signal(barrier, to)
 
+    first, second = pl.ds(0, 128), pl.ds(128, 128)
+
+    def pass_queries(block, half, i, to):
+        ref = qbuf.at[block, c, half]
+        send(ref, ref, q_send.at[i], q_recv.at[i], to)
+
+    def took_queries(i):
+        took(qbuf.at[0, 0, first], q_recv.at[i])
+
+    def share_queries():
+        r, i = iota((256, 256), 0), iota((256, 256), 1)
+        shuffle = ((((r >> 4) & 3) << 6) + ((r >> 6) << 4) + (r & 15) == i).astype(BF16)
+        loads[0].wait()
+        q_hi, q_lo = split(query[...])
+        qbuf[x, c] = mm(shuffle, q_hi, NT) + mm(shuffle, q_lo, NT)
+
+        learn(0, 5)
+        pass_queries(x, first, 0, left)
+        pass_queries(x, second, 1, right)
+        pass_queries(x, second, 2, left)
+        pass_queries(x, first, 3, right)
+        pass_queries(x, first, 6, pair)
+        pass_queries(x, second, 7, pair)
+
+    @pl.when(z < 4)
+    def _():
+        share_queries()
+
     loads[1].wait()
     r, i = iota((64, 64), 0), iota((64, 64), 1)
-    source = (((r >> 2) & 1) << 5) + ((r & 1) << 4) + (((r >> 5) & 1) << 3) + (((r >> 1) & 1) << 2) + ((r >> 3) & 3)
+    source = (((r >> 2) & 1) << 5) + ((r & 3) << 3) + (r >> 3)
     order = (source == i).astype(F32)
     halves = [(iota((64, 128), 1) == iota((64, 128), 0) + 64 * n).astype(F32) for n in range(2)]
     left_inverse = split(
@@ -106,6 +134,10 @@
     )
     loads[2].wait()
     right_inverse = split(jnp.concatenate([exact(binv[n], halves[n], NN) for n in range(2)], axis=0))
+
+    @pl.when(z >= 4)
+    def _():
+        share_queries()
 
     loads[3].wait()
     loads[4].wait()
@@ -116,20 +148,7 @@
         csend[n] = jnp.where(low, both[64 * n : 64 * n + 32], both[64 * n + 32 : 64 * n + 64])
     cbuf[z] = csend[m]
 
-    r, i = iota((256, 256), 0), iota((256, 256), 1)
-    shuffle = ((((r >> 4) & 3) << 6) + ((r >> 6) << 4) + (r & 15) == i).astype(BF16)
-    loads[0].wait()
-    q_hi, q_lo = split(query[...])
-    qbuf[x] = mm(shuffle, q_hi, NT) + mm(shuffle, q_lo, NT)
-
-    learn(1, 5)
-    first, second = pl.ds(0, 128), pl.ds(128, 128)
-    send(qbuf.at[x, first], qbuf.at[x, first], q_send.at[0], q_recv.at[0], left)
-    send(qbuf.at[x, second], qbuf.at[x, second], q_send.at[1], q_recv.at[1], right)
-    send(qbuf.at[x, second], qbuf.at[x, second], q_send.at[2], q_recv.at[2], left)
-    send(qbuf.at[x, first], qbuf.at[x, first], q_send.at[3], q_recv.at[3], right)
-
-    learn(0, 21)
+    learn(1, 21)
     for k in FAR_FIRST:
         send(csend.at[ring(k) // 4], cbuf.at[z], c_sem.at[0], c_sem.at[1], (d, ring(k)))
 
@@ -162,23 +181,25 @@
         lower.append(jnp.where(low, pltpu.roll(even, 64, 1), odd))
     codes_t = split(jnp.concatenate([jnp.concatenate(upper, axis=1), jnp.concatenate(lower, axis=1)], axis=0))
 
-    took(qbuf.at[0, first], q_recv.at[0])
-    after = lax.rem(x + 1, 4)
-    send(qbuf.at[after, first], qbuf.at[after, first], q_send.at[4], q_recv.at[4], left)
-    took(qbuf.at[0, first], q_recv.at[1])
-    before = lax.rem(x + 3, 4)
-    send(qbuf.at[before, second], qbuf.at[before, second], q_send.at[5], q_recv.at[5], right)
-
-    sums = []
+    after, before, beyond = lax.rem(x + 1, 4), lax.rem(x + 3, 4), lax.rem(x + 2, 4)
+    took_queries(0)
+    pass_queries(after, first, 4, left)
+    pass_queries(after, first, 8, pair)
+    took_queries(1)
+    pass_queries(before, second, 5, right)
+    pass_queries(before, second, 9, pair)
+
+    pl.semaphore_wait(ready, len(peers))
+
+    outer = 0.0
     for n in range(CHUNKS):
         took(gbuf.at[n], g_recv.at[n])
-        total = gsend[n, z]
-        for k in range(7):
-            total = total + gbuf[n, k]
-        sums.append(total)
-    columns = jnp.concatenate(sums, axis=1)
-    spread = jnp.concatenate([columns * w for w in weights] * 2, axis=0)
-    outer = mm3(codes_t, split(spread), NT)
+        total = ((gsend[n, z] + gbuf[n, 0]) + (gbuf[n, 1] + gbuf[n, 2])) + ((gbuf[n, 3] + gbuf[n, 4]) + (gbuf[n, 5] + gbuf[n, 6]))
+        at = slice(n * tc, (n + 1) * tc)
+        hi, lo = split(jnp.concatenate([total * w[:, at] for w in weights], axis=0))
+        hi, lo = jnp.concatenate([hi, hi], axis=0), jnp.concatenate([lo, lo], axis=0)
+        c_hi, c_lo = codes_t[0][:, at], codes_t[1][:, at]
+        outer = outer + mm(jnp.concatenate([c_hi, c_lo, c_hi], axis=1), jnp.concatenate([hi, hi, lo], axis=1), NT)
     turned = [outer] + [pltpu.roll(outer, 16 * k, 1) for k in (1, 2, 3)]
     place = iota((8, 128), 1) >> 4
     for g in range(4):
@@ -187,73 +208,73 @@
             piece = jnp.where(place == k, turned[(k - g) % 4][8 * k : 8 * k + 8], piece)
         esend[pl.ds(g, 8, stride=4), :] = piece
 
-    pl.semaphore_wait(ready, len(peers))
-    mine = [[(y == 2 * m + ky) & (c == kc) for kc in range(2)] for ky in range(2)]
     for k in FAR_FIRST + (0,):
-        for ky in range(2):
-            for kc in range(2):
-                y_to, src = 2 * m + ky, esend.at[pl.ds(8 * (2 * ky + kc), 8)]
-                slot = (lax.rem(y - y_to + 4, 4) * 2 + lax.rem(c + kc, 2)) * 4 + jz
-                dst = ebuf.at[slot]
-                to = (dp(y_to, x, kc), ring(k))
-                if k:
+        for n in range(2):
+            y_to = 2 * m + n
+            src = esend.at[pl.ds(16 * n, 16)]
+            dst = ebuf.at[lax.rem(y - y_to + 4, 4) * 4 + jz]
+            to = (dp(y_to, x, c), ring(k))
+            if k:
+                send(src, dst, e_sem.at[0], e_sem.at[1], to)
+            else:
+
+                @pl.when(y != y_to)
+                def _(src=src, dst=dst, to=to):
                     send(src, dst, e_sem.at[0], e_sem.at[1], to)
-                else:
-
-                    @pl.when(jnp.logical_not(mine[ky][kc]))
-                    def _(src=src, dst=dst, to=to):
-                        send(src, dst, e_sem.at[0], e_sem.at[1], to)
-
-                    @pl.when(mine[ky][kc])
-                    def _(src=src, dst=dst):
-                        pltpu.make_async_copy(src, dst, e_sem.at[1]).start()
-
-    def prepare(block, jzs):
-        for n in jzs:
-            hi, lo = split(qbuf[block, pl.ds(64 * n, 64)])
-            at = pl.ds(pl.multiple_of(lax.rem(block, 2) * 64, 64), 64)
-            qhi[block // 2, n, at] = hi
-            qlo[block // 2, n, at] = lo
-
-    prepare(x, range(4))
-    prepare(after, range(2))
-    prepare(before, range(2, 4))
-    took(qbuf.at[0, first], q_recv.at[2])
-    prepare(after, range(2, 4))
-    took(qbuf.at[0, first], q_recv.at[3])
-    prepare(before, range(2))
-    beyond = lax.rem(x + 2, 4)
-    took(qbuf.at[0, first], q_recv.at[4])
-    prepare(beyond, range(2))
-    took(qbuf.at[0, first], q_recv.at[5])
-    prepare(beyond, range(2, 4))
+
+                @pl.when(y == y_to)
+                def _(src=src, dst=dst):
+                    pltpu.make_async_copy(src, dst, e_sem.at[1]).start()
+
+    def prepare(block, core, half):
+        for n in (0, 1) if half is first else (2, 3):
+            hi, lo = split(qbuf[block, core, pl.ds(64 * n, 64)])
+            at = pl.ds(pl.multiple_of(core * 64, 64), 64)
+            qhi[block, n, at] = hi
+            qlo[block, n, at] = lo
+
+    took_queries(2)
+    pass_queries(after, second, 10, pair)
+    took_queries(3)
+    pass_queries(before, first, 11, pair)
+    for block, half in ((x, first), (x, second), (after, first), (before, second), (after, second), (before, first)):
+        prepare(block, c, half)
+    took_queries(4)
+    pass_queries(beyond, first, 12, pair)
+    took_queries(5)
+    pass_queries(beyond, second, 13, pair)
+    prepare(beyond, c, first)
+    prepare(beyond, c, second)
+    for n, (block, half) in enumerate(
+        ((x, first), (x, second), (after, first), (before, second), (after, second), (before, first), (beyond, first), (beyond, second))
+    ):
+        took_queries(6 + n)
+        prepare(block, 1 - c, half)
 
     took(ebuf, e_sem.at[1])
-    pieces = ebuf[...].reshape(8, 4, 8, 128)
+    pieces = ebuf[...].reshape(4, 4, 16, 128)
     e_hi, e_lo = split(jnp.concatenate([pieces[:, n].reshape(64, 128) for n in range(4)], axis=1))
     e_both = jnp.concatenate([e_hi, e_lo], axis=0)
-    part = []
-    for n in range(2):
+    for n in range(4):
         main = mm(e_both, qhi[n].reshape(512, 512), NN)
-        part.append(main[:64] + main[64:] + mm(e_hi, qlo[n].reshape(512, 512), NN))
-    rsum[...] = part[1]
-    for n in range(8):
-        psend[n] = part[0][8 * n : 8 * n + 4] + rsum[8 * n + 4 : 8 * n + 8]
-    for (ky, kc), to in zip(PEERS, peers, strict=True):
-        n = 2 * ky + kc
+        rsum[n] = main[:64] + main[64:] + mm(e_hi, qlo[n].reshape(512, 512), NN)
+    for n in (2, 1, 3, 0):
+        at = [pl.ds(16 * n + 4 * k, 4) for k in range(4)]
+        psend[n] = (rsum[0, at[0]] + rsum[1, at[1]]) + (rsum[2, at[2]] + rsum[3, at[3]])
+    for n, to in zip(PEERS, peers, strict=True):
         send(psend.at[n], pbuf.at[n - 1], p_sem.at[0], p_sem.at[1], to)
     took(pbuf, p_sem.at[1])
     total = psend[0]
-    for n in range(7):
+    for n in range(3):
         total = total + pbuf[n]
     out_ref[...] = total
 
     took(cbuf.at[pl.ds(0, 7)], c_sem.at[0])
     for n in range(CHUNKS):
         took(gbuf.at[n], g_send.at[n])
-    for n in range(6):
-        took(qbuf.at[0, first], q_send.at[n])
-    took(ebuf.at[pl.ds(0, 31)], e_sem.at[0])
+    for n in range(14):
+        took(qbuf.at[0, 0, first], q_send.at[n])
+    took(ebuf.at[pl.ds(0, 15)], e_sem.at[0])
 
     @pl.when(m != y // 2)
     def _():
@@ -268,7 +289,7 @@
     dma, vmem = pltpu.SemaphoreType.DMA, pltpu.VMEM
     return pl.pallas_call(
         kernel,
-        out_shape=jax.ShapeDtypeStruct((4, 512), F32),
+        out_shape=pltpu.VMEM((4, 512), F32),
         in_specs=[pl.BlockSpec(memory_space=pl.ANY)] * 10,
         out_specs=pl.BlockSpec(memory_space=pltpu.VMEM),
         scratch_shapes=[
@@ -286,20 +307,20 @@
             vmem((8, 32, 128), F32),
             vmem((CHUNKS, 8, 16, tc), F32),
             vmem((CHUNKS, 7, 16, tc), F32),
-            vmem((4, 256, 512), F32),
-            vmem((2, 4, 128, 512), BF16),
-            vmem((2, 4, 128, 512), BF16),
+            vmem((4, 2, 256, 512), F32),
+            vmem((4, 4, 128, 512), BF16),
+            vmem((4, 4, 128, 512), BF16),
             vmem((32, 128), F32),
-            vmem((32, 8, 128), F32),
-            vmem((64, 512), F32),
-            vmem((8, 4, 512), F32),
-            vmem((7, 4, 512), F32),
+            vmem((16, 16, 128), F32),
+            vmem((4, 64, 512), F32),
+            vmem((4, 4, 512), F32),
+            vmem((3, 4, 512), F32),
             dma((8 + 2 * CHUNKS,)),
             dma((2,)),
             dma((CHUNKS,)),
             dma((CHUNKS,)),
-            dma((6,)),
-            dma((6,)),
+            dma((14,)),
+            dma((14,)),
             dma((2,)),
             dma((2,)),
             pltpu.SemaphoreType.REGULAR,

time: 33.4 us -> 31.1 us (0.931)
  Pallas kernels: 32 us -> 30.2 us
  local copies, waits for them, and re-layouts: 1.3 us -> 0.6 us
    pallas_call x1, Pallas kernels: 32 us -> 30.2 us  [shards(): pl.pallas_call(kernel, out_shape=pltpu.VMEM((4, 512), F32), in_specs=[pl....]
    unnamed x1, local copies, waits for them, and re-layouts: 1.3 us -> 0.6 us
where the time goes in v4:
time: 31.1 us; the launch traced here: 30.8 us
  Pallas kernels  30.2 us (97%)
  local copies, waits for them, and re-layouts  0.6 us (2%)
    pallas_call x1, Pallas kernels, shards(): pl.pallas_call(kernel, out_shape=pltpu.VMEM((4, 512), F32), in_specs=[pl....  30.2 us

profile of v4, /device:TPU:1, one launch (start us, length us, event | category | flops | bytes accessed | tf_op | source)
XLA Modules:
  0.0 30.8 jit_solution(10855624969383850778)
XLA Ops:
  0.0 30.2 %shard_map.100 = f32[4,512]{1,0:T(4,128)S(1)} custom-call(bf16[64,8192]{1,0:T(8,128)(2,1)} %tokens_hbm.1, bf16[512,3584]{1,0:T(8,128)(2,1)} %gate_hbm.1, bf16[512,3584]{1,0:T(8,128)(2,1)} %up_hbm.1, bf16[8192,128]{1,0:T(8,128)(2,1)} %iproj_hbm.1, bf16[3584,128]{1,0:T(8,128)(2,1)} %oproj_hbm.1, s32[1,512]{1,0:T(1,128)} %bitcast.2, s32[1,4]{1,0:T(1,128)} %bitcast.3, ...), custom_call_target="tpu_custom_call" | custom-call | flops 1000000000 | bytes 12000000 | tf_op jit(solution)/shard_map/pallas_call | solution.py:290
  30.2 0.6 %copy.12 = f32[4,512]{1,0:T(4,128)} copy(f32[4,512]{1,0:T(4,128)S(1)} %shard_map.100) | data formatting | bytes 16384

commit v5 on v4

--- a/solution.py
+++ b/solution.py
@@ -208,23 +208,20 @@
             piece = jnp.where(place == k, turned[(k - g) % 4][8 * k : 8 * k + 8], piece)
         esend[pl.ds(g, 8, stride=4), :] = piece
 
-    for k in FAR_FIRST + (0,):
+    for zt in (0, 2, 1, 3, 4, 7, 5, 6):
         for n in range(2):
             y_to = 2 * m + n
             src = esend.at[pl.ds(16 * n, 16)]
             dst = ebuf.at[lax.rem(y - y_to + 4, 4) * 4 + jz]
-            to = (dp(y_to, x, c), ring(k))
-            if k:
+            own = (y == y_to) & (z == zt)
+
+            @pl.when(jnp.logical_not(own))
+            def _(src=src, dst=dst, to=(dp(y_to, x, c), zt)):
                 send(src, dst, e_sem.at[0], e_sem.at[1], to)
-            else:
-
-                @pl.when(y != y_to)
-                def _(src=src, dst=dst, to=to):
-                    send(src, dst, e_sem.at[0], e_sem.at[1], to)
-
-                @pl.when(y == y_to)
-                def _(src=src, dst=dst):
-                    pltpu.make_async_copy(src, dst, e_sem.at[1]).start()
+
+            @pl.when(own)
+            def _(src=src, dst=dst):
+                pltpu.make_async_copy(src, dst, e_sem.at[1]).start()
 
     def prepare(block, core, half):
         for n in (0, 1) if half is first else (2, 3):
@@ -239,17 +236,18 @@
     pass_queries(before, first, 11, pair)
     for block, half in ((x, first), (x, second), (after, first), (before, second), (after, second), (before, first)):
         prepare(block, c, half)
+    early = ((x, first), (x, second), (after, first), (before, second), (after, second), (before, first))
+    for n, (block, half) in enumerate(early):
+        took_queries(6 + n)
+        prepare(block, 1 - c, half)
     took_queries(4)
     pass_queries(beyond, first, 12, pair)
     took_queries(5)
     pass_queries(beyond, second, 13, pair)
-    prepare(beyond, c, first)
-    prepare(beyond, c, second)
-    for n, (block, half) in enumerate(
-        ((x, first), (x, second), (after, first), (before, second), (after, second), (before, first), (beyond, first), (beyond, second))
-    ):
-        took_queries(6 + n)
-        prepare(block, 1 - c, half)
+    for n, (core, half) in enumerate(((c, first), (c, second), (1 - c, first), (1 - c, second))):
+        if n >= 2:
+            took_queries(10 + n)
+        prepare(beyond, core, half)
 
     took(ebuf, e_sem.at[1])
     pieces = ebuf[...].reshape(4, 4, 16, 128)

time: 31.1 us -> 31.4 us (level)
  no operation moved by 1% of the time
where the time goes in v5:
time: 31.4 us; the launch traced here: 30.8 us
  Pallas kernels  30.2 us (96%)
  local copies, waits for them, and re-layouts  0.6 us (2%)
    pallas_call x1, Pallas kernels, shards(): pl.pallas_call(kernel, out_shape=pltpu.VMEM((4, 512), F32), in_specs=[pl....  30.2 us

profile of v5, /device:TPU:1, one launch (start us, length us, event | category | flops | bytes accessed | tf_op | source)
XLA Modules:
  0.0 30.8 jit_solution(9409022034561494748)
XLA Ops:
  0.0 30.2 %shard_map.100 = f32[4,512]{1,0:T(4,128)S(1)} custom-call(bf16[64,8192]{1,0:T(8,128)(2,1)} %tokens_hbm.1, bf16[512,3584]{1,0:T(8,128)(2,1)} %gate_hbm.1, bf16[512,3584]{1,0:T(8,128)(2,1)} %up_hbm.1, bf16[8192,128]{1,0:T(8,128)(2,1)} %iproj_hbm.1, bf16[3584,128]{1,0:T(8,128)(2,1)} %oproj_hbm.1, s32[1,512]{1,0:T(1,128)} %bitcast.2, s32[1,4]{1,0:T(1,128)} %bitcast.3, ...), custom_call_target="tpu_custom_call" | custom-call | flops 1000000000 | bytes 12000000 | tf_op jit(solution)/shard_map/pallas_call | solution.py:288
  30.2 0.6 %copy.12 = f32[4,512]{1,0:T(4,128)} copy(f32[4,512]{1,0:T(4,128)S(1)} %shard_map.100) | data formatting | bytes 16384
